TPU v7x, 32 devices: a whole 2x2x4 slice. The times are simulated.
32 devices in a mesh: fsdp: 8 (over y, x, core), tp: 4 (over z).
Axes of the slice: x: 2, y: 2, z: 4, core: 2. Of those that a mesh axis runs over, the one named last changes fastest.
Arguments:
- tokens: bfloat16 [4096, 4096], P(('fsdp', 'tp')), may hold values from -6 to 6
- in_weight: bfloat16 [4096, 3, 4096], P('fsdp', None, 'tp'), may hold values from -0.09375 to 0.09375
- out_weight: bfloat16 [4096, 4096], P('fsdp', 'tp'), may hold values from -0.09375 to 0.09375
- short_taps: float32 [3, 3, 4096], P(None, None, 'tp'), may hold values from -3 to 3
- filter_taps: float32 [128, 4096], P(None, 'tp'), may hold values from -1.2 to 1.2
- decay_rate: float32 [4096], P('tp'), may hold values from 0.00390625 to 0.09375
- doc_lengths: int32 [16], replicated, may hold values from 1 to 2048, 4096 in all
Outputs:
- mixed_out: bfloat16 [4096, 4096], P(('fsdp', 'tp'))
Inputs may be any that keep to these rules, and one draw needn't show every extreme that they name: `doc_lengths`: the documents of the window in order; they sum to 4096.
All inputs are finite; a program needn't handle non-finite values.
Results may differ from a plain program's by a relative error of at most 0.014.
Values may be sent and summed in bfloat16 or wider, within the bound.
A program may use at most 128 MiB of HBM per device.

v0:
```python
import jax
import jax.numpy as jnp
from jax import lax
from jax.sharding import PartitionSpec as P


def from_behind(value, axis, by):
    length = lax.axis_size(axis)
    pairs = [(i, i + by) for i in range(length) if 0 <= i + by < length]
    return lax.ppermute(value, axis, pairs)


def doc_position(points, lengths):
    starts = jnp.cumsum(lengths) - lengths
    begins = jnp.max(jnp.where(starts[None, :] <= points[:, None], starts[None, :], 0), axis=1)
    return points - begins


def short_filter(extended, short_taps, positions, out_count):
    running = jnp.zeros((out_count,) + extended.shape[1:], jnp.float32)
    for tap_index in range(3):
        window = extended[2 - tap_index : 2 - tap_index + out_count].astype(jnp.float32)
        inside = (positions >= tap_index)[:, None, None]
        running = running + jnp.where(
            inside, short_taps[tap_index][None] * window, jnp.float32(0.0)
        )
    return running


def long_filter(extended, shaped, positions, out_count, tap_count):

    def tap_group(group_index, running):
        for inner in range(16):
            tap_index = group_index * 16 + inner
            window = lax.dynamic_slice_in_dim(extended, tap_count - tap_index, out_count, 0)
            weight_row = lax.dynamic_slice_in_dim(shaped, tap_index, 1, 0)
            inside = (positions >= tap_index)[:, None]
            running = running + jnp.where(
                inside, weight_row * window.astype(jnp.float32), jnp.float32(0.0)
            )
        return running

    zero_sum = jnp.zeros((out_count, shaped.shape[1]), jnp.float32)
    return lax.fori_loop(0, tap_count // 16, tap_group, zero_sum)


def body(tokens, in_weight, out_weight, short_taps, filter_taps, decay_rate, doc_lengths):
    own_rows = tokens.shape[0]
    slab_count = own_rows * lax.axis_size("tp")
    channels = in_weight.shape[2]
    tap_count = filter_taps.shape[0]
    widened = tokens.astype(jnp.float32)
    normed = (
        widened * lax.rsqrt(jnp.mean(widened * widened, axis=1, keepdims=True) + 1e-06)
    ).astype(jnp.bfloat16)
    gathered = lax.all_gather(normed, "tp", axis=0, tiled=True)
    shard_piece = lax.all_gather(in_weight, "fsdp", axis=0, tiled=True)
    count_rows = shard_piece.shape[0]
    flat_piece = shard_piece.reshape(count_rows, 3 * channels)
    projected = jnp.dot(gathered, flat_piece, preferred_element_type=jnp.float32)
    out_full = lax.all_gather(out_weight, "fsdp", axis=0, tiled=True)
    projected = projected.astype(jnp.bfloat16).reshape(slab_count, 3, channels)
    first_row = lax.axis_index("fsdp") * slab_count
    own_points = first_row + jnp.arange(slab_count, dtype=jnp.int32)
    own_position = doc_position(own_points, doc_lengths)
    edge_rows = from_behind(projected[slab_count - 2 :], "fsdp", 1)
    short_all = short_filter(
        jnp.concatenate([edge_rows, projected], 0), short_taps, own_position, slab_count
    )
    kv_product = (short_all[:, 1] * short_all[:, 2]).astype(jnp.bfloat16)
    tail_rows = from_behind(kv_product[slab_count - tap_count :], "fsdp", 1)
    extended = jnp.concatenate([tail_rows, kv_product], 0)
    query = short_all[:, 0]
    shaped = filter_taps * jnp.exp(
        -decay_rate[None, :] * jnp.arange(tap_count, dtype=jnp.float32)[:, None]
    )
    long_mix = long_filter(extended, shaped, own_position, slab_count, tap_count)
    gated_mix = (query * long_mix).astype(jnp.bfloat16)
    summed = lax.psum_scatter(
        lax.dot_general(
            gated_mix, out_full, (((1,), (1,)), ((), ())), preferred_element_type=jnp.float32
        ).astype(jnp.bfloat16),
        "tp",
        scatter_dimension=0,
        tiled=True,
    ).astype(jnp.float32)
    return (widened + summed).astype(jnp.bfloat16)


def solution(mesh):
    in_specs = (
        P(("fsdp", "tp"), None),
        P("fsdp", None, "tp"),
        P("fsdp", "tp"),
        P(None, None, "tp"),
        P(None, "tp"),
        P("tp"),
        P(),
    )
    out_specs = P(("fsdp", "tp"), None)
    return jax.shard_map(body, mesh=mesh, in_specs=in_specs, out_specs=out_specs, check_vma=False)
```

profile of v0, /device:TPU:0, one launch (start us, length us, event | category | flops | bytes accessed | tf_op | source)
XLA Modules:
  0.0 479.4 jit_solution(16913559615456614631)
XLA Ops:
  6.5 1.7 fusion.16
  8.2 2.5 fusion.17
  10.8 3.0 copy.26
  15.9 78.4 %all-gather.4.cloned.1.call-done = bf16[512,4096]{1,0:T(8,128)(2,1)} async-done(((bf16[128,4096]{1,0:T(8,128)(2,1)}), bf16[512,4096]{1,0:T(8,128)(2,1)}) %all-gather.4.cloned.1.call-update) | async-done | bytes 4194320 | tf_op jit(solution)/shard_map/all_gather | solution.py:56
  94.3 130.7 %all-gather.6.cloned.1.call-done = bf16[4096,3,1024]{0,2,1:T(8,128)(2,1)} async-done(((bf16[512,3,1024]{0,2,1:T(8,128)(2,1)}), bf16[4096,3,1024]{0,2,1:T(8,128)(2,1)}) %all-gather.6.cloned.1.call-update) | async-done | bytes 25165840 | tf_op jit(solution)/shard_map/all_gather | solution.py:57
  225.0 18.2 %convolution_convert_fusion.1 = bf16[512,3072]{1,0:T(8,128)(2,1)S(1)} fusion(bf16[512,4096]{1,0:T(8,128)(2,1)} %all-gather.4.cloned.1.call-done, bf16[4096,3072]{0,1:T(8,128)(2,1)} %bitcast.91), kind=kOutput, calls=%fused_computation.50 | convolution fusion | flops 12886474752 | bytes 32505856 | tf_op jit(solution)/shard_map/dot_general | solution.py:60
  243.2 2.2 collective-permute-start
  245.5 4.7 copy.27
  250.5 9.7 %select_add_fusion.1 = f32[512,3,1024]{0,2,1:T(8,128)S(1)} fusion(bf16[512,3,1024]{0,2,1:T(8,128)(2,1)} %bitcast.72, bf16[2,3,1024]{0,2,1:T(8,128)(2,1)S(1)} %copy.29, f32[3,1024]{1,0:T(4,128)S(1)} %get-tuple-element.291, f32[3,1024]{1,0:T(4,128)S(1)} %get-tuple-element.292, f32[3,1024]{1,0:T(4,128)S(1)} %get-tuple-element.290, ...), kind=kLoop, calls=%fused_computation.48 | loop fusion | flops 26738688 | bytes 9487872 | tf_op jit(solution)/shard_map/add | solution.py:24
  260.7 3.5 collective-permute-start.1
  266.3 1.6 copy.30
  268.0 103.5 %while.17 = (s32[]{:T(128)}, f32[512,1024]{1,0:T(8,128)S(1)}, s32[512]{0:T(512)S(1)}, f32[128,1024]{1,0:T(8,128)}, bf16[640,1024]{1,0:T(8,128)(2,1)S(1)}, /*inde...) while((s32[]{:T(128)}, f32[512,1024]{1,0:T(8,128)S(1)}, ...), condition=%wide.region_4.5_spmd.clone, body=%wide.region_3.4_spmd.clone.sunk | while | flops 34087040 | bytes 21188564 | solution.py:44
  268.1 1.3 constant_dynamic-slice_fusion.17
  269.6 11.2 %fusion.30 = f32[512,1024]{1,0:T(8,128)S(1)} fusion(f32[512,1024]{1,0:T(8,128)S(1)} %get-tuple-element.430, bf16[640,1024]{1,0:T(8,128)(2,1)S(1)} %get-tuple-element.472, s32[]{:T(128)S(6)} %select_n.679, f32[1024]{0:T(1024)S(1)} %bitcast.74, s32[]{:T(128)S(6)} %select_n.696, f32[1024]{0:T(1024)S(1)} %bitcast.75, s32[]{:T(128)S(6)} %select_n.697, ...), kind=kLoop, calls=%fused_computation.15.clone.1 | loop fusion | flops 34078720 | bytes 21045312 | tf_op jit(solution)/shard_map/while/body/eval_jaxpr/add | solution.py:38
  281.0 1.3 constant_dynamic-slice_fusion.17
  282.5 11.2 %fusion.30 = f32[512,1024]{1,0:T(8,128)S(1)} fusion(f32[512,1024]{1,0:T(8,128)S(1)} %get-tuple-element.430, bf16[640,1024]{1,0:T(8,128)(2,1)S(1)} %get-tuple-element.472, s32[]{:T(128)S(6)} %select_n.679, f32[1024]{0:T(1024)S(1)} %bitcast.74, s32[]{:T(128)S(6)} %select_n.696, f32[1024]{0:T(1024)S(1)} %bitcast.75, s32[]{:T(128)S(6)} %select_n.697, ...), kind=kLoop, calls=%fused_computation.15.clone.1 | loop fusion | flops 34078720 | bytes 21045312 | tf_op jit(solution)/shard_map/while/body/eval_jaxpr/add | solution.py:38
  293.9 1.3 constant_dynamic-slice_fusion.17
  295.4 11.2 %fusion.30 = f32[512,1024]{1,0:T(8,128)S(1)} fusion(f32[512,1024]{1,0:T(8,128)S(1)} %get-tuple-element.430, bf16[640,1024]{1,0:T(8,128)(2,1)S(1)} %get-tuple-element.472, s32[]{:T(128)S(6)} %select_n.679, f32[1024]{0:T(1024)S(1)} %bitcast.74, s32[]{:T(128)S(6)} %select_n.696, f32[1024]{0:T(1024)S(1)} %bitcast.75, s32[]{:T(128)S(6)} %select_n.697, ...), kind=kLoop, calls=%fused_computation.15.clone.1 | loop fusion | flops 34078720 | bytes 21045312 | tf_op jit(solution)/shard_map/while/body/eval_jaxpr/add | solution.py:38
  306.8 1.3 constant_dynamic-slice_fusion.17
  308.3 11.2 %fusion.30 = f32[512,1024]{1,0:T(8,128)S(1)} fusion(f32[512,1024]{1,0:T(8,128)S(1)} %get-tuple-element.430, bf16[640,1024]{1,0:T(8,128)(2,1)S(1)} %get-tuple-element.472, s32[]{:T(128)S(6)} %select_n.679, f32[1024]{0:T(1024)S(1)} %bitcast.74, s32[]{:T(128)S(6)} %select_n.696, f32[1024]{0:T(1024)S(1)} %bitcast.75, s32[]{:T(128)S(6)} %select_n.697, ...), kind=kLoop, calls=%fused_computation.15.clone.1 | loop fusion | flops 34078720 | bytes 21045312 | tf_op jit(solution)/shard_map/while/body/eval_jaxpr/add | solution.py:38
  319.7 1.4 constant_dynamic-slice_fusion.17
  321.3 11.2 %fusion.30 = f32[512,1024]{1,0:T(8,128)S(1)} fusion(f32[512,1024]{1,0:T(8,128)S(1)} %get-tuple-element.430, bf16[640,1024]{1,0:T(8,128)(2,1)S(1)} %get-tuple-element.472, s32[]{:T(128)S(6)} %select_n.679, f32[1024]{0:T(1024)S(1)} %bitcast.74, s32[]{:T(128)S(6)} %select_n.696, f32[1024]{0:T(1024)S(1)} %bitcast.75, s32[]{:T(128)S(6)} %select_n.697, ...), kind=kLoop, calls=%fused_computation.15.clone.1 | loop fusion | flops 34078720 | bytes 21045312 | tf_op jit(solution)/shard_map/while/body/eval_jaxpr/add | solution.py:38
  332.6 1.3 constant_dynamic-slice_fusion.17
  334.2 11.2 %fusion.30 = f32[512,1024]{1,0:T(8,128)S(1)} fusion(f32[512,1024]{1,0:T(8,128)S(1)} %get-tuple-element.430, bf16[640,1024]{1,0:T(8,128)(2,1)S(1)} %get-tuple-element.472, s32[]{:T(128)S(6)} %select_n.679, f32[1024]{0:T(1024)S(1)} %bitcast.74, s32[]{:T(128)S(6)} %select_n.696, f32[1024]{0:T(1024)S(1)} %bitcast.75, s32[]{:T(128)S(6)} %select_n.697, ...), kind=kLoop, calls=%fused_computation.15.clone.1 | loop fusion | flops 34078720 | bytes 21045312 | tf_op jit(solution)/shard_map/while/body/eval_jaxpr/add | solution.py:38
  345.5 1.6 constant_dynamic-slice_fusion.17
  347.3 11.2 %fusion.30 = f32[512,1024]{1,0:T(8,128)S(1)} fusion(f32[512,1024]{1,0:T(8,128)S(1)} %get-tuple-element.430, bf16[640,1024]{1,0:T(8,128)(2,1)S(1)} %get-tuple-element.472, s32[]{:T(128)S(6)} %select_n.679, f32[1024]{0:T(1024)S(1)} %bitcast.74, s32[]{:T(128)S(6)} %select_n.696, f32[1024]{0:T(1024)S(1)} %bitcast.75, s32[]{:T(128)S(6)} %select_n.697, ...), kind=kLoop, calls=%fused_computation.15.clone.1 | loop fusion | flops 34078720 | bytes 21045312 | tf_op jit(solution)/shard_map/while/body/eval_jaxpr/add | solution.py:38
  358.7 1.4 constant_dynamic-slice_fusion.17
  360.2 11.2 %fusion.30 = f32[512,1024]{1,0:T(8,128)S(1)} fusion(f32[512,1024]{1,0:T(8,128)S(1)} %get-tuple-element.430, bf16[640,1024]{1,0:T(8,128)(2,1)S(1)} %get-tuple-element.472, s32[]{:T(128)S(6)} %select_n.679, f32[1024]{0:T(1024)S(1)} %bitcast.74, s32[]{:T(128)S(6)} %select_n.696, f32[1024]{0:T(1024)S(1)} %bitcast.75, s32[]{:T(128)S(6)} %select_n.697, ...), kind=kLoop, calls=%fused_computation.15.clone.1 | loop fusion | flops 34078720 | bytes 21045312 | tf_op jit(solution)/shard_map/while/body/eval_jaxpr/add | solution.py:38
  371.5 1.9 copy.31
  373.3 11.3 %convolution_convert_fusion = bf16[512,4096]{1,0:T(8,128)(2,1)} fusion(bf16[4096,1024]{1,0:T(8,128)(2,1)} %all-gather.8.cloned.1.call-done, f32[512,1024]{0,1:T(8,128)} %copy.31, f32[512,3,1024]{0,2,1:T(8,128)} %copy-done), kind=kOutput, calls=%fused_computation.49 | convolution fusion | flops 4298113024 | bytes 16777216 | tf_op jit(solution)/shard_map/dot_general | solution.py:80
  384.6 85.8 %reduce-scatter.2.cloned.1.call-done = bf16[128,4096]{1,0:T(8,128)(2,1)} async-done(((bf16[512,4096]{1,0:T(8,128)(2,1)}), bf16[128,4096]{1,0:T(8,128)(2,1)}) %reduce-scatter.2.cloned.1.call-update) | async-done | bytes 1048592 | tf_op jit(solution)/shard_map/reduce_scatter | solution.py:79
  470.4 2.4 fusion.18
  (54 shorter events, 5.5 us)
Async XLA Ops:
  6.5 4.2 copy-start.3
  6.5 87.8 %all-gather.4.cloned.1.call-start = ((), (), s32[]{:S(2)}) async-start(), calls=%async_computation.1 | async-start | bytes 5242880 | tf_op jit(solution)/shard_map/all_gather | solution.py:56
  10.7 214.3 %all-gather.6.cloned.1.call-start = ((), (), s32[]{:S(2)}) async-start(), calls=%async_computation.2 | async-start | bytes 28311552 | tf_op jit(solution)/shard_map/all_gather | solution.py:57
  13.8 0.8 copy-start.7
  13.8 1.2 copy-start.5
  13.8 1.2 copy-start.6
  13.8 1.2 copy-start.4
  13.8 359.5 %all-gather.8.cloned.1.call-start = ((), (), s32[]{:S(2)}) async-start(), calls=%async_computation.3 | async-start | bytes 9437184 | tf_op jit(solution)/shard_map/all_gather | solution.py:61
  14.5 455.9 %reduce-scatter.2.cloned.1.call-start = ((), (), s32[]{:S(2)}) async-start(), calls=%async_computation.4 | async-start | bytes 5242880 | tf_op jit(solution)/shard_map/reduce_scatter | solution.py:79
  243.2 2.2 copy-start.2
  243.2 6.9 %collective-permute-start = (bf16[2,3,1024]{2,0,1:T(2,128)(2,1)S(1)}, bf16[2,3,1024]{2,0,1:T(2,128)(2,1)S(1)}, u32[]{:S(2)}, u32[]{:S(2)}) collective-permute-start(bf16[2,3,1024]{2,0,1:T(2,128)(2,1)S(1)} %bitcast.89), channel_id=1, source_target_pairs={{0,4},{4,8},{8,12},{12,16},{16,20},{20,24},{24,28},{1,5},{5,9},{9,... | collective-permute-start | bytes 36872 | tf_op jit(solution)/shard_map/ppermute | solution.py:10
  260.3 4.8 %copy-start = (f32[512,3,1024]{0,2,1:T(8,128)}, f32[512,3,1024]{0,2,1:T(8,128)S(1)}, u32[]{:S(2)}) copy-start(f32[512,3,1024]{0,2,1:T(8,128)S(1)} %select_add_fusion.1) | copy-start | bytes 18874372
  260.7 4.4 collective-permute-start.1
  384.6 85.8 %copy-start.1 = (bf16[128,4096]{1,0:T(8,128)(2,1)S(1)}, bf16[128,4096]{1,0:T(8,128)(2,1)}, u32[]{:S(2)}) copy-start(bf16[128,4096]{1,0:T(8,128)(2,1)} %param.9) | copy-start | bytes 3145732
Sparse Core Ops, SparseCore 0:
  10.8 83.4 all-gather.3
  96.2 128.7 all-gather.5
  226.9 56.8 all-gather.7
  384.8 85.6 reduce-scatter.1
where the time goes:
time: 481 us; the launch traced here: 479 us
  waiting for transfers between devices  296 us (62%)
  other arithmetic  110 us (23%)
  matrix products  29.5 us (6%)
  local copies, waits for them, and re-layouts  22.8 us (5%)
  between operations  13.3 us (3%)
  starting transfers between devices  5.76 us (1%)
    all_gather x1, waiting for transfers between devices, body(): shard_piece = lax.all_gather(in_weight, 'fsdp', axis=0, tiled=True)  131 us
    add x8, other arithmetic, tap_group(): running + jnp.where(inside, weight_row * window.astype(jnp.float32), jnp....  90 us
    reduce_scatter x1, waiting for transfers between devices, body(): lax.psum_scatter(lax.dot_general(gated_mix, out_full, (((1,), (1,)), ((),...  85.8 us
    all_gather x1, waiting for transfers between devices, body(): gathered = lax.all_gather(normed, 'tp', axis=0, tiled=True)  78.4 us
    dot_general x1, matrix products, body(): jnp.dot(gathered, flat_piece, preferred_element_type=jnp.float32)  18.2 us
    dot_general x1, matrix products, body(): lax.dot_general(gated_mix, out_full, (((1,), (1,)), ((), ())), preferred_...  11.3 us
    dynamic_slice x8, local copies, waits for them, and re-layouts, tap_group(): weight_row = lax.dynamic_slice_in_dim(shaped, tap_index, 1, 0)  11 us
    add x1, other arithmetic, short_filter(): running + jnp.where(inside, short_taps[tap_index][None] * window, jnp.flo...  9.73 us
  transfers between devices with their start and end apart: 6, of which 4 were waited for; matrix products, arithmetic and copies ran while one was open for 30% of the time, Pallas kernels for 0%

commit v1 on v0

v1 whole, which is shorter than its diff:
```python
import jax
import jax.numpy as jnp
from jax import lax
from jax.experimental import pallas as pl
from jax.experimental.pallas import tpu as pltpu
from jax.sharding import PartitionSpec as P

MESH = pl.DeviceIdType.MESH
HALO = 144


def doc_position(points, lengths):
    starts = jnp.cumsum(lengths) - lengths
    begins = jnp.max(jnp.where(starts[None, :] <= points[:, None], starts[None, :], 0), axis=1)
    return points - begins


def normalize(tokens):
    widened = tokens.astype(jnp.float32)
    return (
        widened * lax.rsqrt(jnp.mean(widened * widened, axis=1, keepdims=True) + 1e-06)
    ).astype(jnp.bfloat16)


def shape_filter(filter_taps, decay_rate):
    tap_count = filter_taps.shape[0]
    return filter_taps * jnp.exp(
        -decay_rate[None, :] * jnp.arange(tap_count, dtype=jnp.float32)[:, None]
    )


def from_behind(value, axis, by):
    length = lax.axis_size(axis)
    pairs = [(i, i + by) for i in range(length) if 0 <= i + by < length]
    return lax.ppermute(value, axis, pairs)


def short_filter(extended, short_taps, positions, out_count):
    running = jnp.zeros((out_count,) + extended.shape[1:], jnp.float32)
    for tap_index in range(3):
        window = extended[2 - tap_index : 2 - tap_index + out_count].astype(jnp.float32)
        inside = (positions >= tap_index)[:, None, None]
        running = running + jnp.where(
            inside, short_taps[tap_index][None] * window, jnp.float32(0.0)
        )
    return running


def long_filter(extended, shaped, positions, out_count, tap_count):
    def tap_group(group_index, running):
        for inner in range(16):
            tap_index = group_index * 16 + inner
            window = lax.dynamic_slice_in_dim(extended, tap_count - tap_index, out_count, 0)
            weight_row = lax.dynamic_slice_in_dim(shaped, tap_index, 1, 0)
            inside = (positions >= tap_index)[:, None]
            running = running + jnp.where(
                inside, weight_row * window.astype(jnp.float32), jnp.float32(0.0)
            )
        return running

    zero_sum = jnp.zeros((out_count, shaped.shape[1]), jnp.float32)
    return lax.fori_loop(0, tap_count // 16, tap_group, zero_sum)


def general_body(tokens, in_weight, out_weight, short_taps, filter_taps, decay_rate, doc_lengths):
    slab_count = tokens.shape[0] * lax.axis_size("tp")
    channels = in_weight.shape[2]
    tap_count = filter_taps.shape[0]
    gathered = lax.all_gather(normalize(tokens), "tp", axis=0, tiled=True)
    shard_piece = lax.all_gather(in_weight, "fsdp", axis=0, tiled=True)
    flat_piece = shard_piece.reshape(shard_piece.shape[0], 3 * channels)
    projected = jnp.dot(gathered, flat_piece, preferred_element_type=jnp.float32)
    out_full = lax.all_gather(out_weight, "fsdp", axis=0, tiled=True)
    projected = projected.astype(jnp.bfloat16).reshape(slab_count, 3, channels)
    first_row = lax.axis_index("fsdp") * slab_count
    own_points = first_row + jnp.arange(slab_count, dtype=jnp.int32)
    own_position = doc_position(own_points, doc_lengths)
    edge_rows = from_behind(projected[slab_count - 2 :], "fsdp", 1)
    short_all = short_filter(
        jnp.concatenate([edge_rows, projected], 0), short_taps, own_position, slab_count
    )
    kv_product = (short_all[:, 1] * short_all[:, 2]).astype(jnp.bfloat16)
    tail_rows = from_behind(kv_product[slab_count - tap_count :], "fsdp", 1)
    extended = jnp.concatenate([tail_rows, kv_product], 0)
    shaped = shape_filter(filter_taps, decay_rate)
    long_mix = long_filter(extended, shaped, own_position, slab_count, tap_count)
    gated_mix = (short_all[:, 0] * long_mix).astype(jnp.bfloat16)
    return finish(tokens, gated_mix, out_full)


def finish(tokens, gated_mix, out_full):
    summed = lax.psum_scatter(
        lax.dot_general(
            gated_mix, out_full, (((1,), (1,)), ((), ())), preferred_element_type=jnp.float32
        ).astype(jnp.bfloat16),
        "tp",
        scatter_dimension=0,
        tiled=True,
    ).astype(jnp.float32)
    return (tokens.astype(jnp.float32) + summed).astype(jnp.bfloat16)


def mix_kernel(
    x_ref, w_ref, o_ref, taps_ref, shaped_ref, pos_ref,
    gated_ref, ofull_ref,
    wbuf, xbuf, pbuf, fbuf, kvbuf, shbuf,
    wsend, wrecv, tsend, trecv, hsend, hrecv, lsem,
):
    chunks, depth, width = w_ref.shape
    cw = width // 3
    rows = x_ref.shape[0]
    f = lax.axis_index("fsdp")
    z = lax.axis_index("tp")
    nf = lax.axis_size("fsdp")
    nz = lax.axis_size("tp")
    slab = rows * nz
    half = depth // 2
    sib = f + 1 - 2 * lax.rem(f, 2)
    xn = f + 2 - 4 * lax.rem(f // 2, 2)
    yn = f + 4 - 8 * (f // 4)
    dn = f + 2 - 4 * lax.rem(f // 2, 2) + 4 - 8 * (f // 4)

    def other(core_of):
        return core_of + 1 - 2 * lax.rem(core_of, 2)

    xbuf[pl.ds(pl.multiple_of(z * rows, rows), rows), :] = x_ref[...]

    @pl.when(f == 0)
    def _():
        for k in range(chunks):
            pbuf[k, 0:HALO, :] = jnp.zeros((HALO, width), pbuf.dtype)

    barrier = pltpu.get_barrier_semaphore()
    for peer in (sib, xn, yn):
        pl.semaphore_signal(barrier, inc=1, device_id=(peer, z), device_id_type=MESH)

    @pl.when(z > 0)
    def _():
        pl.semaphore_signal(barrier, inc=1, device_id=(f, z - 1), device_id_type=MESH)

    @pl.when(z < nz - 1)
    def _():
        pl.semaphore_signal(barrier, inc=1, device_id=(f, z + 1), device_id_type=MESH)

    beside = f - 1 + 2 * lax.rem(f, 2)

    @pl.when(jnp.logical_and(beside >= 0, beside < nf))
    def _():
        pl.semaphore_signal(barrier, inc=1, device_id=(beside, z), device_id_type=MESH)

    peers = (
        3
        + (z + nz - 1) // nz
        + (2 * nz - 2 - z) // nz
        + (f + nf - 1) // nf
        + (2 * nf - 2 - f) // nf
        - 1
    )
    pl.semaphore_wait(barrier, peers)

    def own(p):
        return w_ref.at[p] if p < chunks else o_ref

    def slot(p, origin, part):
        start, size = ((0, depth), (0, half), (half, half))[part]
        at = pl.ds(pl.multiple_of(origin * depth + start, half), size)
        return wbuf.at[p, at] if p < chunks else ofull_ref.at[at]

    def move(p, number, source, origin, part, peer):
        return pltpu.make_async_remote_copy(
            src_ref=source,
            dst_ref=slot(p, origin, part),
            send_sem=wsend.at[p, number],
            recv_sem=wrecv.at[p, number],
            device_id=(peer, z),
            device_id_type=MESH,
        )

    def sends(p):
        return [
            move(p, 0, own(p), f, 0, xn),
            move(p, 1, own(p), f, 0, yn),
            move(p, 2, own(p), f, 0, sib),
            move(p, 3, slot(p, xn, 1), xn, 1, yn),
            move(p, 4, slot(p, yn, 2), yn, 2, xn),
            move(p, 5, slot(p, xn, 0), xn, 0, sib),
            move(p, 6, slot(p, yn, 0), yn, 0, sib),
            move(p, 7, slot(p, dn, 1), dn, 1, sib),
            move(p, 8, slot(p, dn, 2), dn, 2, sib),
        ]

    def arrivals(p):
        where = [
            (xn, 0), (yn, 0), (sib, 0), (dn, 1), (dn, 2),
            (other(xn), 0), (other(yn), 0), (other(dn), 1), (other(dn), 2),
        ]
        return [
            pltpu.make_async_remote_copy(
                src_ref=slot(p, origin, part),
                dst_ref=slot(p, origin, part),
                send_sem=wsend.at[p, number],
                recv_sem=wrecv.at[p, number],
                device_id=(sib, z),
                device_id_type=MESH,
            )
            for number, (origin, part) in enumerate(where)
        ]

    out = [sends(p) for p in range(chunks + 1)]
    come = [arrivals(p) for p in range(chunks + 1)]
    local = [
        pltpu.make_async_copy(own(p), slot(p, f, 0), lsem.at[p]) for p in range(chunks + 1)
    ]

    def launch(p):
        if p <= chunks:
            for number in (0, 1, 2):
                out[p][number].start()
            local[p].start()

    def spread(p):
        if p <= chunks:
            come[p][0].wait_recv()
            out[p][3].start()
            come[p][1].wait_recv()
            out[p][4].start()
            out[p][5].start()
            out[p][6].start()
            launch(p + 2)

    def spread_far(p):
        if p <= chunks:
            come[p][3].wait_recv()
            out[p][7].start()
            come[p][4].wait_recv()
            out[p][8].start()

    def ready(p):
        for number in (2, 5, 6, 7, 8):
            come[p][number].wait_recv()
        local[p].wait()

    def hop(way, step):
        origin = z - step if way == 0 else z + step
        at = pl.ds(pl.multiple_of(origin * rows, rows), rows)
        return pltpu.make_async_remote_copy(
            src_ref=xbuf.at[at],
            dst_ref=xbuf.at[at],
            send_sem=tsend.at[way, step],
            recv_sem=trecv.at[way, step],
            device_id=(f, z + 1 if way == 0 else z - 1),
            device_id_type=MESH,
        )

    def sends_hop(way, step):
        if way == 0:
            return jnp.logical_and(z - step >= 0, z < nz - 1)
        return jnp.logical_and(z + step <= nz - 1, z > 0)

    def gets_hop(way, step):
        return z - 1 - step >= 0 if way == 0 else z + 1 + step <= nz - 1

    def start_hop(step):
        for way in (0, 1):
            @pl.when(sends_hop(way, step))
            def _():
                hop(way, step).start()

    def end_hop(step):
        for way in (0, 1):
            @pl.when(gets_hop(way, step))
            def _():
                origin = z - 1 - step if way == 0 else z + 1 + step
                at = pl.ds(pl.multiple_of(origin * rows, rows), rows)
                pltpu.make_async_remote_copy(
                    src_ref=xbuf.at[at],
                    dst_ref=xbuf.at[at],
                    send_sem=tsend.at[way, step],
                    recv_sem=trecv.at[way, step],
                    device_id=(f, z + 1 if way == 1 else z - 1),
                    device_id_type=MESH,
                ).wait_recv()

    def project(k):
        @pl.loop(0, 3)
        def _(branch):
            at = pl.ds(pl.multiple_of(branch * cw, cw), cw)
            pbuf[k, HALO : HALO + slab, at] = jnp.dot(
                xbuf[...], wbuf[k, :, at], preferred_element_type=jnp.float32
            ).astype(pbuf.dtype)

    def halo(k):
        return pltpu.make_async_remote_copy(
            src_ref=pbuf.at[k, pl.ds(slab, HALO)],
            dst_ref=pbuf.at[k, pl.ds(0, HALO)],
            send_sem=hsend.at[k],
            recv_sem=hrecv.at[k],
            device_id=(f + 1, z),
            device_id_type=MESH,
        )

    def send_halo(k):
        @pl.when(f < nf - 1)
        def _():
            halo(k).start()

    def get_halo(k):
        @pl.when(f > 0)
        def _():
            halo(k).wait_recv()

    ext = slab + 128

    def convolve(k):
        @pl.loop(0, cw // 128)
        def _(lane):
            lanes = pl.ds(pl.multiple_of(k * cw + lane * 128, 128), 128)
            for branch in range(3):
                source = pl.ds(pl.multiple_of(branch * cw + lane * 128, 128), 128)
                fbuf[branch] = pbuf[k, :, source].astype(jnp.float32)

            def short(branch, first, count):
                total = jnp.zeros((count, 128), jnp.float32)
                place = pos_ref[pl.ds(first, count), :]
                for tap in range(3):
                    weight = taps_ref[pl.ds(tap * 3 + branch, 1), lanes]
                    window = fbuf[branch, pl.ds(first - tap, count), :]
                    total = total + jnp.where(place >= tap, weight * window, 0.0)
                return total

            for block in range(ext // 128):
                first = HALO - 128 + block * 128
                product = short(1, first, 128) * short(2, first, 128)
                kvbuf[pl.ds(block * 128, 128), :] = product.astype(jnp.bfloat16).astype(
                    jnp.float32
                )
            for shift in range(8):
                shbuf[shift, pl.ds(8, ext - 8), :] = kvbuf[pl.ds(8 - shift, ext - 8), :]

            for block in range(slab // 128):
                place = pos_ref[pl.ds(HALO + block * 128, 128), :]

                def taps(group, total):
                    weights = shaped_ref[pl.ds(pl.multiple_of(group * 8, 8), 8), lanes]
                    start = pl.multiple_of(128 + block * 128 - group * 8, 8)
                    for shift in range(8):
                        window = shbuf[shift, pl.ds(start, 128), :]
                        total = total + jnp.where(
                            place >= group * 8 + shift,
                            weights[shift : shift + 1, :] * window,
                            0.0,
                        )
                    return total

                mixed = lax.fori_loop(0, 16, taps, jnp.zeros((128, 128), jnp.float32))
                query = short(0, HALO + block * 128, 128)
                gated_ref[pl.ds(block * 128, 128), lanes] = (query * mixed).astype(
                    jnp.bfloat16
                )

    start_hop(0)
    launch(0)
    launch(1)
    spread(0)
    end_hop(0)
    start_hop(1)
    spread_far(0)
    spread(1)
    end_hop(1)
    start_hop(2)
    spread_far(1)
    spread(2)
    end_hop(2)
    ready(0)
    project(0)
    send_halo(0)
    spread_far(2)
    spread(3)
    ready(1)
    project(1)
    send_halo(1)
    spread_far(3)
    spread(4)
    get_halo(0)
    convolve(0)
    spread_far(4)
    for k in range(2, chunks):
        ready(k)
        project(k)
        send_halo(k)
        get_halo(k - 1)
        convolve(k - 1)
    get_halo(chunks - 1)
    convolve(chunks - 1)
    ready(chunks)

    for p in range(chunks + 1):
        for copy in out[p]:
            copy.wait_send()
    for step in range(3):
        for way in (0, 1):
            @pl.when(sends_hop(way, step))
            def _():
                hop(way, step).wait_send()

    @pl.when(f < nf - 1)
    def _():
        for k in range(chunks):
            halo(k).wait_send()


def body(tokens, in_weight, out_weight, short_taps, filter_taps, decay_rate, doc_lengths):
    rows, model = tokens.shape
    depth, _, channels = in_weight.shape
    slab = rows * lax.axis_size("tp")
    nf = lax.axis_size("fsdp")
    chunks = 4
    cw = channels // chunks
    normed = normalize(tokens)
    pieces = in_weight.reshape(depth, 3, chunks, cw).transpose(2, 0, 1, 3).reshape(
        chunks, depth, 3 * cw
    )
    points = (
        lax.axis_index("fsdp") * slab - HALO + jnp.arange(slab + HALO, dtype=jnp.int32)
    )
    position = jnp.broadcast_to(doc_position(points, doc_lengths)[:, None], (slab + HALO, 128))
    shaped = shape_filter(filter_taps, decay_rate)
    vmem = pl.BlockSpec(memory_space=pltpu.VMEM)
    anywhere = pl.BlockSpec(memory_space=pl.ANY)
    gated, out_full = pl.pallas_call(
        mix_kernel,
        out_shape=(
            jax.ShapeDtypeStruct((slab, channels), jnp.bfloat16),
            jax.ShapeDtypeStruct((nf * depth, channels), jnp.bfloat16),
        ),
        in_specs=[vmem, anywhere, anywhere, vmem, vmem, vmem],
        out_specs=(vmem, anywhere),
        scratch_shapes=[
            pltpu.VMEM((chunks, nf * depth, 3 * cw), jnp.bfloat16),
            pltpu.VMEM((slab, model), jnp.bfloat16),
            pltpu.VMEM((chunks, slab + HALO, 3 * cw), jnp.bfloat16),
            pltpu.VMEM((3, slab + HALO, 128), jnp.float32),
            pltpu.VMEM((slab + 128, 128), jnp.float32),
            pltpu.VMEM((8, slab + 128, 128), jnp.float32),
            pltpu.SemaphoreType.DMA((chunks + 1, 9)),
            pltpu.SemaphoreType.DMA((chunks + 1, 9)),
            pltpu.SemaphoreType.DMA((2, 3)),
            pltpu.SemaphoreType.DMA((2, 3)),
            pltpu.SemaphoreType.DMA((chunks,)),
            pltpu.SemaphoreType.DMA((chunks,)),
            pltpu.SemaphoreType.DMA((chunks + 1,)),
        ],
        compiler_params=pltpu.CompilerParams(
            collective_id=0, has_side_effects=True, vmem_limit_bytes=56 * 1024 * 1024
        ),
        cost_estimate=pl.CostEstimate(
            flops=2 * slab * model * 3 * channels,
            bytes_accessed=64 * 1024 * 1024,
            transcendentals=0,
        ),
    )(normed, pieces, out_weight, short_taps.reshape(9, channels), shaped, position)
    return finish(tokens, gated, out_full)


def solution(mesh):
    in_specs = (
        P(("fsdp", "tp"), None),
        P("fsdp", None, "tp"),
        P("fsdp", "tp"),
        P(None, None, "tp"),
        P(None, "tp"),
        P("tp"),
        P(),
    )
    out_specs = P(("fsdp", "tp"), None)
    small = mesh.shape["fsdp"] == 8 and mesh.shape["tp"] == 4
    return jax.shard_map(
        body if small else general_body,
        mesh=mesh,
        in_specs=in_specs,
        out_specs=out_specs,
        check_vma=False,
    )
```

time: 481 us -> 314 us (0.65)
  waiting for transfers between devices: 296 us -> 78.5 us
  Pallas kernels: 0 us -> 190 us
  other arithmetic: 110 us -> 10.1 us
  matrix products: 29.5 us -> 10.2 us
  local copies, waits for them, and re-layouts: 22.8 us -> 11.2 us
  starting transfers between devices: 5.76 us -> 0.01 us
    all_gather x3 -> x0, waiting for transfers between devices: 209 us -> none  [the longest x1 131 us: body(): shard_piece = lax.all_gather(in_weight, 'fsdp', axis=0, tiled=True)]
    pallas_call x0 -> x1, Pallas kernels: none -> 190 us  [body(): pl.pallas_call(mix_kernel, out_shape=(jax.ShapeDtypeStruct((slab, channel...]
    add x10 -> x1, other arithmetic: 99.7 us -> 0.01 us  [body(): lax.axis_index('fsdp') * slab - HALO]
    dot_general x2 -> x1, matrix products: 29.5 us -> 10.2 us  [finish(): lax.dot_general(gated_mix, out_full, (((1,), (1,)), ((), ())), preferred_...]
    dynamic_slice x8 -> x0, local copies, waits for them, and re-layouts: 11 us -> none  [tap_group(): weight_row = lax.dynamic_slice_in_dim(shaped, tap_index, 1, 0)]
    reduce_scatter x1, waiting for transfers between devices: 85.8 us -> 78.5 us  [finish(): lax.psum_scatter(lax.dot_general(gated_mix, out_full, (((1,), (1,)), ((),...]
    ppermute x2 -> x0, starting transfers between devices: 5.63 us -> none  [from_behind(): return lax.ppermute(value, axis, pairs)]
  transfers between devices with their start and end apart: 6 -> 1, of which waited for: 4 -> 1; matrix products, arithmetic and copies ran while one was open for 30% -> 0% of each run, Pallas kernels for 0% -> 0%
where the time goes in v1:
time: 314 us
  Pallas kernels  190 us (61%)
  waiting for transfers between devices  78.5 us (25%)
  between operations  13.4 us (4%)
  local copies, waits for them, and re-layouts  11.2 us (4%)
  matrix products  10.2 us (3%)
  other arithmetic  10.1 us (3%)
    pallas_call x1, Pallas kernels, body(): pl.pallas_call(mix_kernel, out_shape=(jax.ShapeDtypeStruct((slab, channel...  190 us
    reduce_scatter x1, waiting for transfers between devices, finish(): lax.psum_scatter(lax.dot_general(gated_mix, out_full, (((1,), (1,)), ((),...  78.5 us
    dot_general x1, matrix products, finish(): lax.dot_general(gated_mix, out_full, (((1,), (1,)), ((), ())), preferred_...  10.2 us
  transfers between devices with their start and end apart: 1, of which 1 were waited for; matrix products, arithmetic and copies ran while one was open for 0% of the time, Pallas kernels for 0%

profile of v1, /device:TPU:0, one launch (start us, length us, event | category | flops | bytes accessed | tf_op | source)
XLA Modules:
  0.0 313.6 jit_solution(8338208590474053109)
XLA Ops:
  6.5 0.0 copy-start.1
  6.5 0.0 reduce-scatter.2.cloned.1.call-start
  6.5 1.7 fusion
  8.2 0.7 neg.4
  8.9 0.7 copy.18
  9.7 0.1 reduce
  9.8 0.7 sub.14
  10.5 0.1 select_reduce_fusion
  10.6 1.4 reshape.57.taps_ref
  12.0 2.5 fusion.1.x_ref
  14.5 0.0 copy-done.1
  14.5 3.0 copy.16
  17.5 2.3 copy.17
  19.7 2.8 copy.19.w_ref
  22.6 1.9 exponential_multiply_fusion.shaped_ref
  24.5 0.9 broadcast_in_dim.13.pos_ref
  25.4 190.2 %shard_map.73 = (bf16[512,1024]{1,0:T(8,128)(2,1)}, bf16[4096,1024]{1,0:T(8,128)(2,1)}) custom-call(bf16[128,4096]{1,0:T(8,128)(2,1)} %fusion.1.x_ref, bf16[4,512,768]{2,1,0:T(8,128)(2,1)} %copy.19.w_ref, bf16[512,1024]{1,0:T(8,128)(2,1)} %o_ref.1, f32[9,1024]{1,0:T(8,128)} %reshape.57.taps_ref, f32[128,1024]{1,0:T(8,128)} %exponential_multiply_fusion.shaped_ref, ...), custom_call_target="tpu_custom_call" | custom-call | flops 12884901888 | bytes 67108864 | tf_op jit(solution)/shard_map/pallas_call | solution.py:430
  215.6 10.2 %convolution_convert_fusion = bf16[512,4096]{1,0:T(8,128)(2,1)} fusion(bf16[512,1024]{1,0:T(8,128)(2,1)} %get-tuple-element.7, bf16[4096,1024]{1,0:T(8,128)(2,1)} %get-tuple-element.8), kind=kOutput, calls=%fused_computation | convolution fusion | flops 4297064448 | bytes 13631488 | tf_op jit(solution)/shard_map/dot_general | solution.py:93
  225.8 0.0 copy-start
  225.8 0.0 reduce-scatter.2.cloned.1.call-update
  225.9 78.5 %reduce-scatter.2.cloned.1.call-done = bf16[128,4096]{1,0:T(8,128)(2,1)} async-done(((bf16[512,4096]{1,0:T(8,128)(2,1)}), bf16[128,4096]{1,0:T(8,128)(2,1)}) %reduce-scatter.2.cloned.1.call-update) | async-done | bytes 1048592 | tf_op jit(solution)/shard_map/reduce_scatter | solution.py:92
  304.3 0.0 copy-done
  304.3 2.4 fusion.2
  (4 shorter events, 0.1 us)
Async XLA Ops:
  6.5 7.9 %copy-start.1 = (bf16[512,3,1024]{2,0,1:T(8,128)(2,1)S(1)}, bf16[512,3,1024]{2,0,1:T(8,128)(2,1)}, u32[]{:S(2)}) copy-start(bf16[512,3,1024]{2,0,1:T(8,128)(2,1)} %param.8) | copy-start | bytes 9437188
  6.5 297.8 %reduce-scatter.2.cloned.1.call-start = ((), (), s32[]{:S(2)}) async-start(), calls=%async_computation.1 | async-start | bytes 5242880 | tf_op jit(solution)/shard_map/reduce_scatter | solution.py:92
  225.8 78.5 %copy-start = (bf16[128,4096]{1,0:T(8,128)(2,1)S(1)}, bf16[128,4096]{1,0:T(8,128)(2,1)}, u32[]{:S(2)}) copy-start(bf16[128,4096]{1,0:T(8,128)(2,1)} %param.7) | copy-start | bytes 3145732
Sparse Core Ops, SparseCore 0:
  226.0 78.2 reduce-scatter.1

commit v2 on v1

--- a/solution.py
+++ b/solution.py
@@ -101,13 +101,16 @@
 
 
 def mix_kernel(
-    x_ref, w_ref, o_ref, taps_ref, shaped_ref, pos_ref,
-    gated_ref, ofull_ref,
-    wbuf, xbuf, pbuf, fbuf, kvbuf, shbuf,
-    wsend, wrecv, tsend, trecv, hsend, hrecv, lsem,
+    len_ref, x_ref, w_ref, o_ref, taps_ref, filter_ref, decay_ref,
+    out_ref,
+    gated_ref, ofull_ref, shaped_ref, pos_ref,
+    wbuf, xbuf, pbuf, fbuf, kvbuf, shbuf, rbuf, sums,
+    wsend, wrecv, tsend, trecv, hsend, hrecv, lsem, rsend, rrecv,
 ):
-    chunks, depth, width = w_ref.shape
+    depth = w_ref.shape[1]
+    chunks, _, width = wbuf.shape
     cw = width // 3
+    tap_count = filter_ref.shape[0]
     rows = x_ref.shape[0]
     f = lax.axis_index("fsdp")
     z = lax.axis_index("tp")
@@ -123,12 +126,49 @@
     def other(core_of):
         return core_of + 1 - 2 * lax.rem(core_of, 2)
 
-    xbuf[pl.ds(pl.multiple_of(z * rows, rows), rows), :] = x_ref[...]
+    @pl.loop(0, rows // 16)
+    def _(group):
+        at = pl.ds(pl.multiple_of(group * 16, 16), 16)
+        put = pl.ds(pl.multiple_of(z * rows + group * 16, 16), 16)
+        xbuf[put, :] = normalize(x_ref[at, :])
+
+    for first in range(0, HALO + slab, 16):
+        point = f * slab - HALO + first + lax.broadcasted_iota(jnp.int32, (16, 128), 0)
+        start = jnp.int32(0)
+        begins = jnp.zeros((16, 128), jnp.int32)
+        for doc in range(len_ref.shape[0]):
+            begins = jnp.maximum(begins, jnp.where(start <= point, start, 0))
+            start = start + len_ref[doc]
+        pos_ref[first : first + 16, :] = point - begins
+
+    @pl.loop(0, tap_count // 8)
+    def _(group):
+        at = pl.ds(pl.multiple_of(group * 8, 8), 8)
+        tap = (group * 8 + lax.broadcasted_iota(jnp.int32, (8, decay_ref.shape[1]), 0)).astype(
+            jnp.float32
+        )
+        shaped_ref[at, :] = filter_ref[at, :] * jnp.exp(-decay_ref[...] * tap)
 
     @pl.when(f == 0)
     def _():
         for k in range(chunks):
             pbuf[k, 0:HALO, :] = jnp.zeros((HALO, width), pbuf.dtype)
+
+    mine = pl.ds(pl.multiple_of(f * depth, depth), depth)
+    local = [
+        [
+            pltpu.make_async_copy(
+                w_ref.at[branch, :, pl.ds(p * cw, cw)],
+                wbuf.at[p, mine, pl.ds(branch * cw, cw)],
+                lsem.at[p, branch],
+            )
+            for branch in range(3)
+        ]
+        for p in range(chunks)
+    ] + [[pltpu.make_async_copy(o_ref, ofull_ref.at[mine], lsem.at[chunks, 0])]]
+    for piece in local:
+        for copy in piece:
+            copy.start()
 
     barrier = pltpu.get_barrier_semaphore()
     for peer in (sib, xn, yn):
@@ -158,9 +198,6 @@
     )
     pl.semaphore_wait(barrier, peers)
 
-    def own(p):
-        return w_ref.at[p] if p < chunks else o_ref
-
     def slot(p, origin, part):
         start, size = ((0, depth), (0, half), (half, half))[part]
         at = pl.ds(pl.multiple_of(origin * depth + start, half), size)
@@ -178,9 +215,9 @@
 
     def sends(p):
         return [
-            move(p, 0, own(p), f, 0, xn),
-            move(p, 1, own(p), f, 0, yn),
-            move(p, 2, own(p), f, 0, sib),
+            move(p, 0, slot(p, f, 0), f, 0, xn),
+            move(p, 1, slot(p, f, 0), f, 0, yn),
+            move(p, 2, slot(p, f, 0), f, 0, sib),
             move(p, 3, slot(p, xn, 1), xn, 1, yn),
             move(p, 4, slot(p, yn, 2), yn, 2, xn),
             move(p, 5, slot(p, xn, 0), xn, 0, sib),
@@ -208,15 +245,13 @@
 
     out = [sends(p) for p in range(chunks + 1)]
     come = [arrivals(p) for p in range(chunks + 1)]
-    local = [
-        pltpu.make_async_copy(own(p), slot(p, f, 0), lsem.at[p]) for p in range(chunks + 1)
-    ]
 
     def launch(p):
         if p <= chunks:
+            for copy in local[p]:
+                copy.wait()
             for number in (0, 1, 2):
                 out[p][number].start()
-            local[p].start()
 
     def spread(p):
         if p <= chunks:
@@ -238,7 +273,6 @@
     def ready(p):
         for number in (2, 5, 6, 7, 8):
             come[p][number].wait_recv()
-        local[p].wait()
 
     def hop(way, step):
         origin = z - step if way == 0 else z + step
@@ -323,7 +357,7 @@
                 total = jnp.zeros((count, 128), jnp.float32)
                 place = pos_ref[pl.ds(first, count), :]
                 for tap in range(3):
-                    weight = taps_ref[pl.ds(tap * 3 + branch, 1), lanes]
+                    weight = taps_ref[tap, pl.ds(branch, 1), lanes]
                     window = fbuf[branch, pl.ds(first - tap, count), :]
                     total = total + jnp.where(place >= tap, weight * window, 0.0)
                 return total
@@ -357,6 +391,80 @@
                 gated_ref[pl.ds(block * 128, 128), lanes] = (query * mixed).astype(
                     jnp.bfloat16
                 )
+
+    columns = 2 * depth
+    pairs = [f // 2, xn // 2, yn // 2, dn // 2]
+
+    def part(owner, q):
+        at = pl.ds(pl.multiple_of(pairs[q] * columns, columns), columns)
+        return lax.dot_general(
+            gated_ref[pl.ds(pl.multiple_of(owner * rows, rows), rows), :],
+            ofull_ref[at, :],
+            (((1,), (1,)), ((), ())),
+            preferred_element_type=jnp.float32,
+        )
+
+    def carry(way, step, q):
+        return pltpu.make_async_remote_copy(
+            src_ref=rbuf.at[way, step, q],
+            dst_ref=rbuf.at[way, step, q],
+            send_sem=rsend.at[way, step, q],
+            recv_sem=rrecv.at[way, step, q],
+            device_id=(f, z + 1 if way == 0 else z - 1),
+            device_id_type=MESH,
+        )
+
+    def arrive(way, step, q):
+        pltpu.make_async_remote_copy(
+            src_ref=rbuf.at[way, step, q],
+            dst_ref=rbuf.at[way, step, q],
+            send_sem=rsend.at[way, step, q],
+            recv_sem=rrecv.at[way, step, q],
+            device_id=(f, z - 1 if way == 0 else z + 1),
+            device_id_type=MESH,
+        ).wait_recv()
+
+    def carries(way, step):
+        return nz - 1 - step > z if way == 0 else step < z
+
+    def has_before(way):
+        return z > 0 if way == 0 else z < nz - 1
+
+    def pass_sums(q):
+        for step in range(3):
+            for way in (0, 1):
+                owner = 3 - step if way == 0 else step
+
+                @pl.when(carries(way, step))
+                def _():
+                    value = part(owner, q)
+
+                    @pl.when(has_before(way))
+                    def _():
+                        arrive(way, step, q)
+                        rbuf[way, step, q] = (
+                            value + rbuf[way, step, q].astype(jnp.float32)
+                        ).astype(jnp.bfloat16)
+
+                    @pl.when(jnp.logical_not(has_before(way)))
+                    def _():
+                        rbuf[way, step, q] = value.astype(jnp.bfloat16)
+
+                    carry(way, step, q).start()
+
+    def settle(q):
+        at = pl.ds(pl.multiple_of(pairs[q] * columns, columns), columns)
+        sums[...] = part(z, q) + x_ref[:, at].astype(jnp.float32)
+        for step in range(3):
+            for way in (0, 1):
+                here = z == nz - 1 - step if way == 0 else z == step
+
+                @pl.when(here)
+                def _():
+                    arrive(way, step, q)
+                    sums[...] = sums[...] + rbuf[way, step, q].astype(jnp.float32)
+
+        out_ref[:, at] = sums[...].astype(jnp.bfloat16)
 
     start_hop(0)
     launch(0)
@@ -375,24 +483,47 @@
     project(0)
     send_halo(0)
     spread_far(2)
-    spread(3)
     ready(1)
     project(1)
     send_halo(1)
-    spread_far(3)
-    spread(4)
     get_halo(0)
     convolve(0)
+    spread(3)
+    ready(2)
+    project(2)
+    send_halo(2)
+    get_halo(1)
+    convolve(1)
+    spread_far(3)
+    ready(3)
+    project(3)
+    send_halo(3)
+    get_halo(2)
+    convolve(2)
+    spread(4)
+    get_halo(3)
+    convolve(3)
+    come[chunks][2].wait_recv()
+    pass_sums(0)
     spread_far(4)
-    for k in range(2, chunks):
-        ready(k)
-        project(k)
-        send_halo(k)
-        get_halo(k - 1)
-        convolve(k - 1)
-    get_halo(chunks - 1)
-    convolve(chunks - 1)
-    ready(chunks)
+    come[chunks][5].wait_recv()
+    pass_sums(1)
+    settle(0)
+    come[chunks][6].wait_recv()
+    pass_sums(2)
+    settle(1)
+    come[chunks][7].wait_recv()
+    come[chunks][8].wait_recv()
+    pass_sums(3)
+    settle(2)
+    settle(3)
+
+    for step in range(3):
+        for way in (0, 1):
+            @pl.when(carries(way, step))
+            def _():
+                for q in range(4):
+                    carry(way, step, q).wait_send()
 
     for p in range(chunks + 1):
         for copy in out[p]:
@@ -416,50 +547,55 @@
     nf = lax.axis_size("fsdp")
     chunks = 4
     cw = channels // chunks
-    normed = normalize(tokens)
-    pieces = in_weight.reshape(depth, 3, chunks, cw).transpose(2, 0, 1, 3).reshape(
-        chunks, depth, 3 * cw
-    )
-    points = (
-        lax.axis_index("fsdp") * slab - HALO + jnp.arange(slab + HALO, dtype=jnp.int32)
-    )
-    position = jnp.broadcast_to(doc_position(points, doc_lengths)[:, None], (slab + HALO, 128))
-    shaped = shape_filter(filter_taps, decay_rate)
     vmem = pl.BlockSpec(memory_space=pltpu.VMEM)
     anywhere = pl.BlockSpec(memory_space=pl.ANY)
-    gated, out_full = pl.pallas_call(
+    return pl.pallas_call(
         mix_kernel,
-        out_shape=(
-            jax.ShapeDtypeStruct((slab, channels), jnp.bfloat16),
-            jax.ShapeDtypeStruct((nf * depth, channels), jnp.bfloat16),
-        ),
-        in_specs=[vmem, anywhere, anywhere, vmem, vmem, vmem],
-        out_specs=(vmem, anywhere),
+        out_shape=jax.ShapeDtypeStruct((rows, model), jnp.bfloat16),
+        in_specs=[
+            pl.BlockSpec(memory_space=pltpu.SMEM), vmem, anywhere, anywhere, vmem, vmem, vmem,
+        ],
+        out_specs=vmem,
         scratch_shapes=[
+            pltpu.VMEM((slab, channels), jnp.bfloat16),
+            pltpu.VMEM((nf * depth, channels), jnp.bfloat16),
+            pltpu.VMEM(filter_taps.shape, jnp.float32),
+            pltpu.VMEM((slab + HALO, 128), jnp.int32),
             pltpu.VMEM((chunks, nf * depth, 3 * cw), jnp.bfloat16),
             pltpu.VMEM((slab, model), jnp.bfloat16),
             pltpu.VMEM((chunks, slab + HALO, 3 * cw), jnp.bfloat16),
             pltpu.VMEM((3, slab + HALO, 128), jnp.float32),
             pltpu.VMEM((slab + 128, 128), jnp.float32),
             pltpu.VMEM((8, slab + 128, 128), jnp.float32),
+            pltpu.VMEM((2, 3, 4, rows, 2 * depth), jnp.bfloat16),
+            pltpu.VMEM((rows, 2 * depth), jnp.float32),
             pltpu.SemaphoreType.DMA((chunks + 1, 9)),
             pltpu.SemaphoreType.DMA((chunks + 1, 9)),
             pltpu.SemaphoreType.DMA((2, 3)),
             pltpu.SemaphoreType.DMA((2, 3)),
             pltpu.SemaphoreType.DMA((chunks,)),
             pltpu.SemaphoreType.DMA((chunks,)),
-            pltpu.SemaphoreType.DMA((chunks + 1,)),
+            pltpu.SemaphoreType.DMA((chunks + 1, 3)),
+            pltpu.SemaphoreType.DMA((2, 3, 4)),
+            pltpu.SemaphoreType.DMA((2, 3, 4)),
         ],
         compiler_params=pltpu.CompilerParams(
-            collective_id=0, has_side_effects=True, vmem_limit_bytes=56 * 1024 * 1024
+            collective_id=0, has_side_effects=True, vmem_limit_bytes=62 * 1024 * 1024
         ),
         cost_estimate=pl.CostEstimate(
-            flops=2 * slab * model * 3 * channels,
-            bytes_accessed=64 * 1024 * 1024,
+            flops=2 * slab * model * 4 * channels,
+            bytes_accessed=16 * 1024 * 1024,
             transcendentals=0,
         ),
-    )(normed, pieces, out_weight, short_taps.reshape(9, channels), shaped, position)
-    return finish(tokens, gated, out_full)
+    )(
+        doc_lengths,
+        tokens,
+        in_weight.transpose(1, 0, 2),
+        out_weight,
+        short_taps,
+        filter_taps,
+        decay_rate[None, :],
+    )
 
 
 def solution(mesh):

time: 314 us -> 279 us (0.89)
  Pallas kernels: 190 us -> 277 us
  waiting for transfers between devices: 78.5 us -> 0 us
  between operations: 13.4 us -> 0.01 us
  matrix products: 10.2 us -> 0 us
  other arithmetic: 10.1 us -> 0 us
  local copies, waits for them, and re-layouts: 11.2 us -> 2.29 us
    pallas_call x1, Pallas kernels: 190 us -> 277 us  [body(): pl.pallas_call(mix_kernel, out_shape=jax.ShapeDtypeStruct((rows, model),...]
    reduce_scatter x1 -> x0, waiting for transfers between devices: 78.5 us -> none  [finish(): lax.psum_scatter(lax.dot_general(gated_mix, out_full, (((1,), (1,)), ((),...]
    dot_general x1 -> x0, matrix products: 10.2 us -> none  [finish(): lax.dot_general(gated_mix, out_full, (((1,), (1,)), ((), ())), preferred_...]
    convert_element_type x2 -> x0, other arithmetic: 4.9 us -> none  [the longest x1 2.45 us: normalize(): return (widened * lax.rsqrt(jnp.mean(widened * widened, axis=1, keepdims=...]
    reshape x2 -> x0, local copies, waits for them, and re-layouts: 4.28 us -> none  [the longest x1 2.84 us: body(): in_weight.reshape(depth, 3, chunks, cw).transpose(2, 0, 1, 3)]
  transfers between devices with their start and end apart: 1 -> 0, of which waited for: 1 -> 0; matrix products, arithmetic and copies ran while one was open for 0% -> 0% of each run, Pallas kernels for 0% -> 0%
where the time goes in v2:
time: 279 us
  Pallas kernels  277 us (99%)
    pallas_call x1, Pallas kernels, body(): pl.pallas_call(mix_kernel, out_shape=jax.ShapeDtypeStruct((rows, model),...  277 us

profile of v2, /device:TPU:0, one launch (start us, length us, event | category | flops | bytes accessed | tf_op | source)
XLA Modules:
  0.0 279.1 jit_solution(14636554900041135961)
XLA Ops:
  0.0 276.8 %shard_map.73 = bf16[128,4096]{1,0:T(8,128)(2,1)} custom-call(s32[16]{0:T(128)} %len_ref.1, bf16[128,4096]{1,0:T(8,128)(2,1)} %x_ref.1, bf16[3,512,1024]{2,1,0:T(8,128)(2,1)} %bitcast.2, bf16[512,1024]{1,0:T(8,128)(2,1)} %o_ref.1, f32[3,3,1024]{2,1,0:T(4,128)} %taps_ref.1, f32[128,1024]{1,0:T(8,128)} %filter_ref.1, f32[1,1024]{1,0:T(1,128)} %bitcast.3), custom_call_target="tpu_custom_call" | custom-call | flops 17179869184 | bytes 16777216 | tf_op jit(solution)/shard_map/pallas_call | solution.py:552
  276.8 2.3 copy.9

commit v3 on v2

--- a/solution.py
+++ b/solution.py
@@ -368,25 +368,42 @@
                 kvbuf[pl.ds(block * 128, 128), :] = product.astype(jnp.bfloat16).astype(
                     jnp.float32
                 )
-            for shift in range(8):
-                shbuf[shift, pl.ds(8, ext - 8), :] = kvbuf[pl.ds(8 - shift, ext - 8), :]
+            for shift in range(16):
+                shbuf[shift, pl.ds(16, ext - 16), :] = kvbuf[
+                    pl.ds(16 - shift, ext - 16), :
+                ].astype(jnp.bfloat16)
 
             for block in range(slab // 128):
-                place = pos_ref[pl.ds(HALO + block * 128, 128), :]
-
-                def taps(group, total):
-                    weights = shaped_ref[pl.ds(pl.multiple_of(group * 8, 8), 8), lanes]
-                    start = pl.multiple_of(128 + block * 128 - group * 8, 8)
-                    for shift in range(8):
-                        window = shbuf[shift, pl.ds(start, 128), :]
-                        total = total + jnp.where(
-                            place >= group * 8 + shift,
-                            weights[shift : shift + 1, :] * window,
-                            0.0,
-                        )
-                    return total
-
-                mixed = lax.fori_loop(0, 16, taps, jnp.zeros((128, 128), jnp.float32))
+                first = (
+                    jnp.minimum(pos_ref[pl.ds(HALO + block * 128, 128), :], 128)
+                    .astype(jnp.float32)
+                    .astype(jnp.bfloat16)
+                    .reshape(8, 16, 128)
+                )
+
+                def taps(group, carried):
+                    place, total = carried
+                    weights = shaped_ref[pl.ds(pl.multiple_of(group * 16, 16), 16), lanes]
+                    start = pl.multiple_of(128 + block * 128 - group * 16, 16)
+                    for first_shift in (0, 8):
+                        few = jnp.zeros((8, 16, 128), jnp.bfloat16)
+                        for shift in range(first_shift, first_shift + 8):
+                            window = shbuf[shift, pl.ds(start, 128), :].reshape(8, 16, 128)
+                            weight = jnp.broadcast_to(
+                                weights[shift : shift + 1, :], (16, 128)
+                            ).astype(jnp.bfloat16)
+                            few = few + jnp.where(
+                                place >= jnp.bfloat16(shift),
+                                weight[None] * window,
+                                jnp.bfloat16(0.0),
+                            )
+                        total = total + few.astype(jnp.float32)
+                    return place - jnp.bfloat16(16.0), total
+
+                _, mixed = lax.fori_loop(
+                    0, 8, taps, (first, jnp.zeros((8, 16, 128), jnp.float32))
+                )
+                mixed = mixed.reshape(128, 128)
                 query = short(0, HALO + block * 128, 128)
                 gated_ref[pl.ds(block * 128, 128), lanes] = (query * mixed).astype(
                     jnp.bfloat16
@@ -566,7 +583,7 @@
             pltpu.VMEM((chunks, slab + HALO, 3 * cw), jnp.bfloat16),
             pltpu.VMEM((3, slab + HALO, 128), jnp.float32),
             pltpu.VMEM((slab + 128, 128), jnp.float32),
-            pltpu.VMEM((8, slab + 128, 128), jnp.float32),
+            pltpu.VMEM((16, slab + 128, 128), jnp.bfloat16),
             pltpu.VMEM((2, 3, 4, rows, 2 * depth), jnp.bfloat16),
             pltpu.VMEM((rows, 2 * depth), jnp.float32),
             pltpu.SemaphoreType.DMA((chunks + 1, 9)),

time: 279 us -> 263 us (0.943)
  Pallas kernels: 277 us -> 261 us
    pallas_call x1, Pallas kernels: 277 us -> 261 us  [body(): pl.pallas_call(mix_kernel, out_shape=jax.ShapeDtypeStruct((rows, model),...]
where the time goes in v3:
time: 263 us
  Pallas kernels  261 us (99%)
    pallas_call x1, Pallas kernels, body(): pl.pallas_call(mix_kernel, out_shape=jax.ShapeDtypeStruct((rows, model),...  261 us

profile of v3, /device:TPU:0, one launch (start us, length us, event | category | flops | bytes accessed | tf_op | source)
XLA Modules:
  0.0 262.9 jit_solution(10837105289328369129)
XLA Ops:
  0.0 260.6 %shard_map.73 = bf16[128,4096]{1,0:T(8,128)(2,1)} custom-call(s32[16]{0:T(128)} %len_ref.1, bf16[128,4096]{1,0:T(8,128)(2,1)} %x_ref.1, bf16[3,512,1024]{2,1,0:T(8,128)(2,1)} %bitcast.2, bf16[512,1024]{1,0:T(8,128)(2,1)} %o_ref.1, f32[3,3,1024]{2,1,0:T(4,128)} %taps_ref.1, f32[128,1024]{1,0:T(8,128)} %filter_ref.1, f32[1,1024]{1,0:T(1,128)} %bitcast.3), custom_call_target="tpu_custom_call" | custom-call | flops 17179869184 | bytes 16777216 | tf_op jit(solution)/shard_map/pallas_call | solution.py:569
  260.7 2.3 copy.9
